TPU v7x, 32 devices: a whole 2x2x4 slice. The times are simulated.
32 devices in a mesh: dp: 8 (over z, core), pos: 4 (over y, x).
Axes of the slice: x: 2, y: 2, z: 4, core: 2. Of those that a mesh axis runs over, the one named last changes fastest.
Arguments:
- features: bfloat16 [64, 128, 224], P(('dp', 'pos')), may hold values from -6 to 6
- counts: int32 [32], P(('dp', 'pos')), may hold values from 1 to 2, as said below
- channel_order: int32 [224], replicated, may hold values from 0 to 223, each once
Outputs:
- mean: float32 [128, 100], P('pos')
- covariance: float32 [128, 100, 100], P('pos')
Inputs may be any that keep to these rules, and one draw needn't show every extreme that they name: `counts`: some device has all 2 slots live and some device only one.
All inputs are finite; a program needn't handle non-finite values.
Results may differ from a plain program's by a relative error of at most 0.0003.
Values may be sent and summed in bfloat16 or wider, within the bound.
No kernel may reach another device: no remote copies, remote signals or barrier semaphores. Data moves between devices by JAX's collectives and lax.ppermute only.
A program may use at most 128 MiB of HBM per device.

v0:
```python
import jax
import jax.numpy as jnp
from jax import lax
from jax.sharding import PartitionSpec as P

CH = 100


def local_stats(received, source_counts, slots, rows, width):
    sources = source_counts.shape[0]
    samples = received.reshape(sources * slots, rows, width).astype(jnp.float32)
    live_mask = (jnp.arange(slots, dtype=jnp.float32)[None, :] < source_counts[:, None]).astype(
        jnp.float32
    )
    live_mask = live_mask.reshape(sources * slots)
    group_count = jnp.sum(source_counts).reshape(1)
    group_sums = jnp.sum(samples, axis=0)
    group_mean = group_sums / group_count
    centered = (samples - group_mean[None]) * live_mask[:, None, None]
    products = jnp.einsum("gpc,gpd->pcd", centered, centered, precision=lax.Precision.HIGHEST)
    return (group_count, group_sums, group_mean, products)


def common_mean(group_count, group_sums, group_mean):
    total_count, total_sums = lax.psum((group_count, group_sums), "dp")
    mean = total_sums / total_count
    offset = group_mean - mean
    weighted = offset * group_count
    return (total_count, mean, offset, weighted)


def on_device(features, counts, channel_order):
    slots, positions, channels = features.shape
    groups = lax.axis_size("pos")
    pos_dev = positions // groups
    kept = channel_order[:CH]
    picker = (kept[None, :] == jnp.arange(channels, dtype=jnp.int32)[:, None]).astype(jnp.bfloat16)
    owned = counts[0]
    slot_live = (jnp.arange(slots, dtype=jnp.int32) < owned).astype(jnp.bfloat16)
    embed = jnp.dot(
        features.reshape(slots * positions, channels), picker, preferred_element_type=jnp.float32
    )
    embed = embed.astype(jnp.bfloat16).reshape(slots, positions, CH) * slot_live[:, None, None]
    identity = jnp.eye(CH, dtype=jnp.float32)
    packed = embed.reshape(slots, groups, pos_dev * CH)
    owned_wire = jnp.broadcast_to(owned.astype(jnp.bfloat16).reshape(1, 1, 1), (1, groups, 1))
    received, source_counts = (
        lax.all_to_all(packed, "pos", split_axis=1, concat_axis=0, tiled=True),
        lax.all_to_all(owned_wire, "pos", split_axis=1, concat_axis=0, tiled=True),
    )
    source_counts = source_counts.reshape(groups).astype(jnp.float32)
    group_count, group_sums, group_mean, products = local_stats(
        received, source_counts, slots, pos_dev, CH
    )
    total_count, mean, offset, weighted = common_mean(group_count, group_sums, group_mean)
    own_term = products + offset[:, :, None] * weighted[:, None, :]
    summed = lax.psum(own_term, "dp")
    covariance = summed / (total_count[0] - 1.0) + 0.01 * identity
    return (mean, covariance)


def solution(mesh):
    in_specs = (P(("dp", "pos"), None, None), P(("dp", "pos")), P())
    out_specs = (P("pos", None), P("pos", None, None))
    return jax.shard_map(
        on_device, mesh=mesh, in_specs=in_specs, out_specs=out_specs, check_vma=False
    )
```

profile of v0, /device:TPU:0, one launch (start us, length us, event | category | flops | bytes accessed | tf_op | source)
XLA Modules:
  0.0 129.7 jit_solution(13337276662901932767)
XLA Ops:
  7.2 0.0 copy-start
  7.9 0.6 broadcast_in_dim.2
  8.4 5.2 %all-to-all-start.1 = ((bf16[1,4,1]{2,0,1:T(2,128)(2,1)}), bf16[1,4,1]{2,0,1:T(2,128)(2,1)S(1)}, u32[]{:S(2)}, u32[]{:S(2)}) async-start(bf16[1,4,1]{2,0,1:T(2,128)(2,1)} %broadcast_in_dim.2), calls=%async_computation.1 | async-start | bytes 4096 | tf_op jit(solution)/shard_map/all_to_all | solution.py:49
  13.6 0.7 slice.3
  14.3 0.0 copy-done
  14.3 0.2 fusion
  14.5 0.1 copy.19
  14.6 0.2 reshape.81
  14.8 0.1 broadcast_multiply_fusion
  14.9 0.7 copy.20
  15.6 2.6 %all-to-all-done.1 = bf16[1,4,1]{2,0,1:T(2,128)(2,1)S(1)} async-done(((bf16[1,4,1]{2,0,1:T(2,128)(2,1)}), bf16[1,4,1]{2,0,1:T(2,128)(2,1)S(1)}, u32[]{:S(2)}, u32[]{:S(2)}) %all-to-all-start.1) | async-done | bytes 40 | tf_op jit(solution)/shard_map/all_to_all | solution.py:49
  18.2 3.3 %all-to-all-start = ((bf16[2,4,3200]{2,0,1:T(2,128)(2,1)}), bf16[2,4,3200]{2,0,1:T(2,128)(2,1)S(1)}, u32[]{:S(2)}, u32[]{:S(2)}) async-start(bf16[2,4,3200]{2,0,1:T(2,128)(2,1)} %copy.20), calls=%async_computation | async-start | bytes 102400 | tf_op jit(solution)/shard_map/all_to_all | solution.py:48
  21.5 0.0 all-reduce.3.cloned.1.call-start
  21.5 0.7 convert_reduce_fusion.1
  22.2 0.1 fusion.6
  22.3 0.1 reshape.85
  22.4 3.9 %all-to-all-done = bf16[2,4,3200]{2,0,1:T(2,128)(2,1)S(1)} async-done(((bf16[2,4,3200]{2,0,1:T(2,128)(2,1)}), bf16[2,4,3200]{2,0,1:T(2,128)(2,1)S(1)}, u32[]{:S(2)}, u32[]{:S(2)}) %all-to-all-start) | async-done | bytes 51232 | tf_op jit(solution)/shard_map/all_to_all | solution.py:48
  26.2 0.1 convert_reduce_fusion
  26.3 0.1 reduce_sum.21
  26.5 0.3 reshape.84
  26.7 27.4 %all-reduce = (f32[32,100]{1,0:T(8,128)S(1)}, f32[]{:T(128)}) all-reduce(f32[32,100]{1,0:T(8,128)S(1)} %reduce_sum.21, f32[]{:T(128)} %get-tuple-element.11), channel_id=1, replica_groups=mesh['dp'=8,'pos'=4] {'dp'}, use_global_device_ids=true, to_apply=%region_1.0 | all-reduce | flops 3201 | bytes 25608 | tf_op jit(solution)/shard_map/psum | solution.py:25
  54.2 1.9 %broadcast_multiply_fusion.1 = (f32[32,100]{1,0:T(8,128)S(1)}, f32[32,100]{1,0:T(8,128)S(1)}, f32[32,100]{1,0:T(8,128)S(1)}, f32[32,100]{1,0:T(8,128)}) fusion(f32[]{:T(128)} %get-tuple-element.11, f32[32,100]{1,0:T(8,128)S(1)} %reduce_sum.21, f32[32,100]{1,0:T(8,128)S(1)} %get-tuple-element.12, f32[]{:T(128)} %get-tuple-element.13), kind=kLoop, calls=%fused_computation.15 | loop fusion | flops 12800 | bytes 76808 | tf_op jit(solution)/shard_map/mul | solution.py:28
  56.1 0.1 subtract_multiply_fusion
  56.2 4.4 %multiply_add_fusion = f32[32,100,100]{2,1,0:T(8,128)} fusion(f32[32,100]{1,0:T(8,128)S(1)} %get-tuple-element.14, f32[32,100]{1,0:T(8,128)S(1)} %get-tuple-element.15, f32[8,32,100]{2,1,0:T(8,128)S(1)} %subtract_multiply_fusion), kind=kOutput, calls=%fused_computation.1 | convolution fusion | flops 31360000 | bytes 1408000 | tf_op jit(solution)/shard_map/gpc,gpd->pcd/dot_general | solution.py:20
  60.6 0.0 all-reduce.3.cloned.1.call-update
  61.3 58.5 %all-reduce.3.cloned.1.call-done = f32[32,100,100]{2,1,0:T(8,128)} async-done(((f32[32,100,100]{2,1,0:T(8,128)}), f32[32,100,100]{2,1,0:T(8,128)}) %all-reduce.3.cloned.1.call-update) | async-done | bytes 1280016 | tf_op jit(solution)/shard_map/psum | solution.py:57
  119.8 1.6 %divide_add_fusion = f32[32,100,100]{2,1,0:T(8,128)S(1)} fusion(f32[32,100,100]{2,1,0:T(8,128)} %all-reduce.3.cloned.1.call-done, f32[100,100]{1,0:T(8,128)S(1)} %fusion.5, f32[]{:T(128)S(6)} %sub.17), kind=kLoop, calls=%fused_computation | loop fusion | flops 640000 | bytes 2600004 | tf_op jit(solution)/shard_map/add | solution.py:58
  121.4 1.5 %copy.23 = f32[32,100,100]{2,0,1:T(8,128)} copy(f32[32,100,100]{2,1,0:T(8,128)S(1)} %divide_add_fusion) | data formatting | bytes 2560000
  (3 shorter events, 0.1 us)
Async XLA Ops:
  7.2 7.1 %copy-start = (bf16[2,128,224]{1,2,0:T(8,128)(2,1)S(1)}, bf16[2,128,224]{1,2,0:T(8,128)(2,1)}, u32[]{:S(2)}) copy-start(bf16[2,128,224]{1,2,0:T(8,128)(2,1)} %param.3) | copy-start | bytes 344068
  8.4 9.7 %all-to-all-start.1 = ((bf16[1,4,1]{2,0,1:T(2,128)(2,1)}), bf16[1,4,1]{2,0,1:T(2,128)(2,1)S(1)}, u32[]{:S(2)}, u32[]{:S(2)}) async-start(bf16[1,4,1]{2,0,1:T(2,128)(2,1)} %broadcast_in_dim.2), calls=%async_computation.1 | async-start | bytes 4096 | tf_op jit(solution)/shard_map/all_to_all | solution.py:49
  18.2 8.1 %all-to-all-start = ((bf16[2,4,3200]{2,0,1:T(2,128)(2,1)}), bf16[2,4,3200]{2,0,1:T(2,128)(2,1)S(1)}, u32[]{:S(2)}, u32[]{:S(2)}) async-start(bf16[2,4,3200]{2,0,1:T(2,128)(2,1)} %copy.20), calls=%async_computation | async-start | bytes 102400 | tf_op jit(solution)/shard_map/all_to_all | solution.py:48
  21.5 98.3 %all-reduce.3.cloned.1.call-start = ((), (), s32[]{:S(2)}) async-start(), calls=%async_computation.2 | async-start | bytes 3407872 | tf_op jit(solution)/shard_map/psum | solution.py:57
Sparse Core Ops, SparseCore 0:
  60.7 59.0 all-reduce.2
where the time goes:
time: 130 us
  waiting for transfers between devices  65 us (50%)
  blocking collectives  27.4 us (21%)
  between operations  15.4 us (12%)
  starting transfers between devices  8.48 us (7%)
  other arithmetic  4.59 us (4%)
  matrix products  4.57 us (4%)
  local copies, waits for them, and re-layouts  4.13 us (3%)
    psum x1, waiting for transfers between devices, on_device(): summed = lax.psum(own_term, 'dp')  58.5 us
    psum x1, blocking collectives, common_mean(): total_count, total_sums = lax.psum((group_count, group_sums), 'dp')  27.4 us
    all_to_all x1, starting transfers between devices, on_device(): lax.all_to_all(owned_wire, 'pos', split_axis=1, concat_axis=0, tiled=True)  5.16 us
    dot_general x1, matrix products, local_stats(): jnp.einsum('gpc,gpd->pcd', centered, centered, precision=lax.Precision.HI...  4.36 us
    all_to_all x1, waiting for transfers between devices, on_device(): lax.all_to_all(packed, 'pos', split_axis=1, concat_axis=0, tiled=True)  3.88 us
    all_to_all x1, starting transfers between devices, on_device(): lax.all_to_all(packed, 'pos', split_axis=1, concat_axis=0, tiled=True)  3.28 us
    all_to_all x1, waiting for transfers between devices, on_device(): lax.all_to_all(owned_wire, 'pos', split_axis=1, concat_axis=0, tiled=True)  2.61 us
  transfers between devices with their start and end apart: 3, of which 3 were waited for; matrix products, arithmetic and copies ran while one was open for 2% of the time, Pallas kernels for 0%

commit v1 on v0

--- a/solution.py
+++ b/solution.py
@@ -4,6 +4,29 @@
 from jax.sharding import PartitionSpec as P
 
 CH = 100
+
+
+def in_blocks(x, dim, size):
+    before, after = (x.shape[:dim], x.shape[dim + 1 :])
+    return jnp.moveaxis(x.reshape(*before, size, -1, *after), dim, 0)
+
+
+def laid_out(parts, dim):
+    lengths = list(parts.shape[1:])
+    lengths[dim] *= parts.shape[0]
+    return jnp.moveaxis(parts, 0, dim).reshape(lengths)
+
+
+def rotated_exchange(value, axis, split_dim, concat_dim):
+    size, place = (lax.axis_size(axis), lax.axis_index(axis))
+    parts = in_blocks(value, split_dim, size)
+    out = parts
+    for lap in range(1, size):
+        target, source = ((place + lap) % size, (place - lap) % size)
+        sent = lax.dynamic_index_in_dim(parts, target, 0)
+        received = lax.ppermute(sent, axis, [(i, (i + lap) % size) for i in range(size)])
+        out = lax.dynamic_update_slice_in_dim(out, received, source, axis=0)
+    return laid_out(out, concat_dim)
 
 
 def local_stats(received, source_counts, slots, rows, width):
@@ -46,7 +69,7 @@
     owned_wire = jnp.broadcast_to(owned.astype(jnp.bfloat16).reshape(1, 1, 1), (1, groups, 1))
     received, source_counts = (
         lax.all_to_all(packed, "pos", split_axis=1, concat_axis=0, tiled=True),
-        lax.all_to_all(owned_wire, "pos", split_axis=1, concat_axis=0, tiled=True),
+        rotated_exchange(owned_wire, "pos", 1, 0),
     )
     source_counts = source_counts.reshape(groups).astype(jnp.float32)
     group_count, group_sums, group_mean, products = local_stats(

time: 130 us -> 132 us (1.015)
  starting transfers between devices: 8.48 us -> 13.2 us
  waiting for transfers between devices: 65 us -> 60.6 us
  local copies, waits for them, and re-layouts: 4.13 us -> 5.72 us
    ppermute x0 -> x3, starting transfers between devices: none -> 9.83 us  [rotated_exchange(): lax.ppermute(sent, axis, [(i, (i + lap) % size) for i in range(size)])]
    all_to_all x1 -> x0, starting transfers between devices: 5.16 us -> none  [on_device(): lax.all_to_all(owned_wire, 'pos', split_axis=1, concat_axis=0, tiled=True)]
    all_to_all x1 -> x0, waiting for transfers between devices: 2.61 us -> none  [on_device(): lax.all_to_all(owned_wire, 'pos', split_axis=1, concat_axis=0, tiled=True)]
    all_to_all x1, waiting for transfers between devices: 3.88 us -> 1.62 us  [on_device(): lax.all_to_all(packed, 'pos', split_axis=1, concat_axis=0, tiled=True)]
    dynamic_update_slice x0 -> x3, local copies, waits for them, and re-layouts: none -> 2.17 us  [rotated_exchange(): out = lax.dynamic_update_slice_in_dim(out, received, source, axis=0)]
  transfers between devices with their start and end apart: 3 -> 5, of which waited for: 3 -> 2; matrix products, arithmetic and copies ran while one was open for 2% -> 4% of each run, Pallas kernels for 0% -> 0%
where the time goes in v1:
time: 132 us; the launch traced here: 131 us
  waiting for transfers between devices  60.6 us (46%)
  blocking collectives  27.2 us (21%)
  between operations  15.5 us (12%)
  starting transfers between devices  13.2 us (10%)
  local copies, waits for them, and re-layouts  5.72 us (4%)
  other arithmetic  4.6 us (3%)
  matrix products  4.57 us (3%)
    psum x1, waiting for transfers between devices, on_device(): summed = lax.psum(own_term, 'dp')  58.9 us
    psum x1, blocking collectives, common_mean(): total_count, total_sums = lax.psum((group_count, group_sums), 'dp')  27.2 us
    ppermute x3, starting transfers between devices, rotated_exchange(): lax.ppermute(sent, axis, [(i, (i + lap) % size) for i in range(size)])  9.83 us
    dot_general x1, matrix products, local_stats(): jnp.einsum('gpc,gpd->pcd', centered, centered, precision=lax.Precision.HI...  4.37 us
    all_to_all x1, starting transfers between devices, on_device(): lax.all_to_all(packed, 'pos', split_axis=1, concat_axis=0, tiled=True)  3.28 us
  transfers between devices with their start and end apart: 5, of which 2 were waited for; matrix products, arithmetic and copies ran while one was open for 4% of the time, Pallas kernels for 0%

profile of v1, /device:TPU:0, one launch (start us, length us, event | category | flops | bytes accessed | tf_op | source)
XLA Modules:
  0.0 131.3 jit_solution(15129336794907413112)
XLA Ops:
  7.2 0.0 copy-start
  7.9 4.3 %collective-permute-start = (bf16[1,1,1,1]{3,2,1,0:T(2,128)(2,1)}, bf16[1,1,1,1]{3,2,1,0:T(2,128)(2,1)}, u32[]{:S(2)}, u32[]{:S(2)}) collective-permute-start(bf16[1,1,1,1]{3,2,1,0:T(2,128)(2,1)} %bitcast.2), channel_id=1, source_target_pairs={{0,1},{1,2},{2,3},{3,0},{4,5},{5,6},{6,7},{7,4},{8,9},{9,10},{10,1... | collective-permute-start | bytes 14 | tf_op jit(solution)/shard_map/ppermute | solution.py:27
  12.2 2.8 %collective-permute-start.1 = (bf16[1,1,1,1]{3,2,1,0:T(2,128)(2,1)}, bf16[1,1,1,1]{3,2,1,0:T(2,128)(2,1)}, u32[]{:S(2)}, u32[]{:S(2)}) collective-permute-start(bf16[1,1,1,1]{3,2,1,0:T(2,128)(2,1)} %bitcast.2), channel_id=1, source_target_pairs={{0,2},{1,3},{2,0},{3,1},{4,6},{5,7},{6,4},{7,5},{8,10},{9,11},{10,... | collective-permute-start | bytes 14 | tf_op jit(solution)/shard_map/ppermute | solution.py:27
  15.0 2.7 %collective-permute-start.2 = (bf16[1,1,1,1]{3,2,1,0:T(2,128)(2,1)}, bf16[1,1,1,1]{3,2,1,0:T(2,128)(2,1)}, u32[]{:S(2)}, u32[]{:S(2)}) collective-permute-start(bf16[1,1,1,1]{3,2,1,0:T(2,128)(2,1)} %bitcast.2), channel_id=1, source_target_pairs={{0,3},{1,0},{2,1},{3,2},{4,7},{5,4},{6,5},{7,6},{8,11},{9,8},{10,9... | collective-permute-start | bytes 14 | tf_op jit(solution)/shard_map/ppermute | solution.py:27
  17.7 0.7 slice.3
  18.4 0.0 copy-done
  18.4 0.2 fusion
  18.6 0.1 copy.13
  18.7 0.2 reshape.79
  18.9 0.1 broadcast_multiply_fusion
  19.0 0.7 copy.14
  19.7 3.3 %all-to-all-start = ((bf16[2,4,3200]{2,0,1:T(2,128)(2,1)}), bf16[2,4,3200]{2,0,1:T(2,128)(2,1)S(1)}, u32[]{:S(2)}, u32[]{:S(2)}) async-start(bf16[2,4,3200]{2,0,1:T(2,128)(2,1)} %copy.14), calls=%async_computation | async-start | bytes 102400 | tf_op jit(solution)/shard_map/all_to_all | solution.py:71
  22.9 0.0 all-reduce.3.cloned.1.call-start
  23.1 0.0 collective-permute-done
  23.1 0.7 dynamic_update_slice.12
  23.8 0.0 collective-permute-done.1
  23.8 0.7 dynamic_update_slice.13
  24.6 0.0 collective-permute-done.2
  24.6 0.7 dynamic_update_slice.14
  25.3 0.1 fusion.6
  25.3 0.7 convert_reduce_fusion.1
  26.0 0.1 reshape.83
  26.1 1.6 %all-to-all-done = bf16[2,4,3200]{2,0,1:T(2,128)(2,1)S(1)} async-done(((bf16[2,4,3200]{2,0,1:T(2,128)(2,1)}), bf16[2,4,3200]{2,0,1:T(2,128)(2,1)S(1)}, u32[]{:S(2)}, u32[]{:S(2)}) %all-to-all-start) | async-done | bytes 51232 | tf_op jit(solution)/shard_map/all_to_all | solution.py:71
  27.7 0.1 convert_reduce_fusion
  27.8 0.1 reduce_sum.21
  27.9 0.3 reshape.82
  28.2 27.2 %all-reduce = (f32[32,100]{1,0:T(8,128)S(1)}, f32[]{:T(128)}) all-reduce(f32[32,100]{1,0:T(8,128)S(1)} %reduce_sum.21, f32[]{:T(128)} %convert_reduce_fusion.1), channel_id=1, replica_groups=mesh['dp'=8,'pos'=4] {'dp'}, use_global_device_ids=true, to_apply=%region_1.2 | all-reduce | flops 3201 | bytes 25608 | tf_op jit(solution)/shard_map/psum | solution.py:48
  55.4 1.9 %broadcast_multiply_fusion.1 = (f32[32,100]{1,0:T(8,128)S(1)}, f32[32,100]{1,0:T(8,128)S(1)}, f32[32,100]{1,0:T(8,128)S(1)}, f32[32,100]{1,0:T(8,128)}) fusion(f32[]{:T(128)} %convert_reduce_fusion.1, f32[32,100]{1,0:T(8,128)S(1)} %reduce_sum.21, f32[32,100]{1,0:T(8,128)S(1)} %get-tuple-element.8, f32[]{:T(128)} %get-tuple-element.9), kind=kLoop, calls=%fused_computation.15 | loop fusion | flops 12800 | bytes 76808 | tf_op jit(solution)/shard_map/mul | solution.py:51
  57.3 0.1 subtract_multiply_fusion
  57.4 4.4 %multiply_add_fusion = f32[32,100,100]{2,1,0:T(8,128)} fusion(f32[32,100]{1,0:T(8,128)S(1)} %get-tuple-element.10, f32[32,100]{1,0:T(8,128)S(1)} %get-tuple-element.11, f32[8,32,100]{2,1,0:T(8,128)S(1)} %subtract_multiply_fusion), kind=kOutput, calls=%fused_computation.1 | convolution fusion | flops 31360000 | bytes 1408000 | tf_op jit(solution)/shard_map/gpc,gpd->pcd/dot_general | solution.py:43
  61.8 0.0 all-reduce.3.cloned.1.call-update
  62.5 58.9 %all-reduce.3.cloned.1.call-done = f32[32,100,100]{2,1,0:T(8,128)} async-done(((f32[32,100,100]{2,1,0:T(8,128)}), f32[32,100,100]{2,1,0:T(8,128)}) %all-reduce.3.cloned.1.call-update) | async-done | bytes 1280016 | tf_op jit(solution)/shard_map/psum | solution.py:80
  121.4 1.6 %divide_add_fusion = f32[32,100,100]{2,1,0:T(8,128)S(1)} fusion(f32[32,100,100]{2,1,0:T(8,128)} %all-reduce.3.cloned.1.call-done, f32[100,100]{1,0:T(8,128)S(1)} %fusion.5, f32[]{:T(128)S(6)} %sub.29), kind=kLoop, calls=%fused_computation | loop fusion | flops 640000 | bytes 2600004 | tf_op jit(solution)/shard_map/add | solution.py:81
  123.0 1.5 %copy.17 = f32[32,100,100]{2,0,1:T(8,128)} copy(f32[32,100,100]{2,1,0:T(8,128)S(1)} %divide_add_fusion) | data formatting | bytes 2560000
  (5 shorter events, 0.1 us)
Async XLA Ops:
  7.2 11.2 %copy-start = (bf16[2,128,224]{1,2,0:T(8,128)(2,1)S(1)}, bf16[2,128,224]{1,2,0:T(8,128)(2,1)}, u32[]{:S(2)}) copy-start(bf16[2,128,224]{1,2,0:T(8,128)(2,1)} %param.3) | copy-start | bytes 344068
  7.9 15.2 %collective-permute-start = (bf16[1,1,1,1]{3,2,1,0:T(2,128)(2,1)}, bf16[1,1,1,1]{3,2,1,0:T(2,128)(2,1)}, u32[]{:S(2)}, u32[]{:S(2)}) collective-permute-start(bf16[1,1,1,1]{3,2,1,0:T(2,128)(2,1)} %bitcast.2), channel_id=1, source_target_pairs={{0,1},{1,2},{2,3},{3,0},{4,5},{5,6},{6,7},{7,4},{8,9},{9,10},{10,1... | collective-permute-start | bytes 14 | tf_op jit(solution)/shard_map/ppermute | solution.py:27
  12.2 11.7 %collective-permute-start.1 = (bf16[1,1,1,1]{3,2,1,0:T(2,128)(2,1)}, bf16[1,1,1,1]{3,2,1,0:T(2,128)(2,1)}, u32[]{:S(2)}, u32[]{:S(2)}) collective-permute-start(bf16[1,1,1,1]{3,2,1,0:T(2,128)(2,1)} %bitcast.2), channel_id=1, source_target_pairs={{0,2},{1,3},{2,0},{3,1},{4,6},{5,7},{6,4},{7,5},{8,10},{9,11},{10,... | collective-permute-start | bytes 14 | tf_op jit(solution)/shard_map/ppermute | solution.py:27
  15.0 9.6 %collective-permute-start.2 = (bf16[1,1,1,1]{3,2,1,0:T(2,128)(2,1)}, bf16[1,1,1,1]{3,2,1,0:T(2,128)(2,1)}, u32[]{:S(2)}, u32[]{:S(2)}) collective-permute-start(bf16[1,1,1,1]{3,2,1,0:T(2,128)(2,1)} %bitcast.2), channel_id=1, source_target_pairs={{0,3},{1,0},{2,1},{3,2},{4,7},{5,4},{6,5},{7,6},{8,11},{9,8},{10,9... | collective-permute-start | bytes 14 | tf_op jit(solution)/shard_map/ppermute | solution.py:27
  19.7 8.1 %all-to-all-start = ((bf16[2,4,3200]{2,0,1:T(2,128)(2,1)}), bf16[2,4,3200]{2,0,1:T(2,128)(2,1)S(1)}, u32[]{:S(2)}, u32[]{:S(2)}) async-start(bf16[2,4,3200]{2,0,1:T(2,128)(2,1)} %copy.14), calls=%async_computation | async-start | bytes 102400 | tf_op jit(solution)/shard_map/all_to_all | solution.py:71
  22.9 98.5 %all-reduce.3.cloned.1.call-start = ((), (), s32[]{:S(2)}) async-start(), calls=%async_computation.1 | async-start | bytes 3407872 | tf_op jit(solution)/shard_map/psum | solution.py:80
Sparse Core Ops, SparseCore 0:
  61.9 59.4 all-reduce.2
